TPU v7x, 32 devices: a whole 2x2x4 slice. The times are simulated.
32 devices in a mesh: pb: 4 (over y, x), db: 8 (over z, core).
Axes of the slice: x: 2, y: 2, z: 4, core: 2. Of those that a mesh axis runs over, the one named last changes fastest.
Arguments:
- database: bfloat16 [2048, 768], P('db')
- neighbours: int32 [2048, 16], P('db'), may hold values from 0 to 2047, as said below
- valid_count: int32 [2048], P('db'), may hold values from 9 to 16, as said below
- queries: bfloat16 [65536, 768], P('pb'), may hold values from -6 to 6
Outputs:
- augmented: bfloat16 [2048, 768], P('db')
- best_score: float32 [65536], P('pb')
Inputs may be any that keep to these rules, and one draw needn't show every extreme that they name: `neighbours`: every entry is a row number of the whole database, also in slots at or past valid_count (those carry no weight). The owner of row r is r // 256. In each aligned block of 64 rows, at most 256 of its 1024 entries name rows of one owner, and in every block some owner is named by exactly 256 entries. `valid_count`: every aligned block of 64 rows holds a row with 16 valid slots.
All inputs are finite; a program needn't handle non-finite values.
Results may differ from a plain program's by a relative error of at most 0.0028.
Values may be sent and summed in bfloat16 or wider, within the bound.
No kernel may reach another device: no remote copies, remote signals or barrier semaphores. Data moves between devices by JAX's collectives and lax.ppermute only.
A program may use at most 128 MiB of HBM per device.

v0:
```python
import functools

import jax
import jax.numpy as jnp
from jax import lax
from jax.experimental import pallas as pl
from jax.experimental.pallas import tpu as pltpu
from jax.sharding import PartitionSpec as P

epsilon = 1e-06
MIB = 1 << 20


def column_inverse(values):
    squares = jnp.sum(values * values, axis=-1, keepdims=True)
    return lax.rsqrt(squares + epsilon)


def as_row(column):
    wide = jnp.broadcast_to(column, (column.shape[0], 128))
    return wide.T[0:1, :]


def position_of():
    owner = lax.axis_index("db")
    return lax.axis_index("pb"), owner // 2, owner % 2


def fetch_queries(queries_ref, held_ref, part, sem):
    rows = held_ref.shape[0]
    core = position_of()[2]
    start = pl.multiple_of((core * 2 + part) * rows, rows)
    return pltpu.make_async_copy(queries_ref.at[pl.ds(start, rows), :], held_ref, sem)


def count_kernel(
    planes, twin_ref, own_ref, database_ref, queries_ref, early_ref, middle_ref, late_ref, copy_ref, held_ref,
    tiles_ref, lows_ref, sem, queries_sem,
):
    rows = copy_ref.shape[0]
    fanout = own_ref.shape[0] * 128 // rows
    quarter = rows // 4
    span = (planes - 1) * quarter
    early_tiles = early_ref.shape[1] // 128
    middle_tiles = middle_ref.shape[1] // 128
    late_tiles = late_ref.shape[1] // 128
    cut = span // 2
    copy = pltpu.make_async_copy(database_ref, copy_ref, sem)
    copy.start()
    queries = fetch_queries(queries_ref, held_ref, 0, queries_sem)
    queries.start()
    me, plane, core = position_of()
    bits = rows.bit_length() - 1
    lines = own_ref.shape[0]
    for number, wanted_ref in enumerate((twin_ref, own_ref)):
        wanted = wanted_ref[...]
        owner = wanted >> bits
        side = owner & 1
        row = wanted & (rows - 1)
        cross = (row >> (bits - 2)) ^ me
        inner = row & (quarter - 1)
        away = (owner >> 1) ^ plane
        paired = (cross == 3) & (away > 1)
        held = jnp.where(paired, away & 1, side) == core
        straight = (away - 1) * quarter
        crossed = ((away >> 1) * 2 - 1 + (side ^ core)) * quarter
        middle = early_tiles * 128
        late = middle + middle_tiles * 128
        straight = straight + inner
        crossed = crossed + inner
        second = jnp.where(cross == 1 + core, 0, cut)
        forwarded = straight + second + jnp.where(straight < cut, middle, late + span - cut)
        position = jnp.where(cross == 3, late + jnp.where(paired, crossed, straight), forwarded)
        position = jnp.where(cross == 0, rows + straight, position)
        position = jnp.where(away == 0, row, position)
        position = jnp.where((wanted >= 0) & held, position, -1)
        tiles_ref[number * lines : (number + 1) * lines, :] = position >> 7
        lows_ref[number * lines : (number + 1) * lines, :] = position & 127

    group = 16
    height = (early_tiles + middle_tiles + late_tiles) * group
    width = group * fanout
    at_row = lax.broadcasted_iota(jnp.int32, (height, width), 0)
    at_lane = lax.broadcasted_iota(jnp.int32, (height, width), 1)
    target = jnp.where(at_lane // fanout == at_row % group, at_row // group, -2)
    low_of = lax.broadcasted_iota(jnp.int32, (128, width), 0)
    each = width // 128

    def flat(ref, at):
        return jnp.concatenate([ref[pl.ds(at * each + i, 1), :] for i in range(each)], axis=1)

    def body(at, carry):
        tile = jnp.broadcast_to(flat(tiles_ref, at), (height, width))
        low = jnp.broadcast_to(flat(lows_ref, at), (128, width))
        left = jnp.where(tile == target, 1.0, 0.0).astype(jnp.bfloat16)
        right = jnp.where(low == low_of, 1.0, 0.0).astype(jnp.bfloat16)
        counts = lax.dot_general(
            left, right, (((1,), (1,)), ((), ())), preferred_element_type=jnp.float32
        ).astype(jnp.bfloat16)
        start = pl.ds(pl.multiple_of(at * group, group), group)
        tile = 0
        for count_ref in (early_ref, middle_ref, late_ref):
            for t in range(count_ref.shape[1] // 128):
                count_ref[start, t * 128 : (t + 1) * 128] = counts[tile * group : (tile + 1) * group, :]
                tile += 1
        return carry

    lax.fori_loop(0, 2 * rows // group, body, 0, unroll=4)
    copy.wait()
    queries.wait()


def join_kernel(own_ref, twin_ref, *rest):
    both_ref, alone_ref, first_ref, second_ref = rest[-4:]
    quarter = alone_ref.shape[0]
    me = position_of()[0]
    at = pl.multiple_of((me ^ 3) * quarter, quarter)
    both_ref[:quarter, :] = own_ref[pl.ds(at, quarter), :]
    both_ref[quarter:, :] = twin_ref[pl.ds(at, quarter), :]
    alone_ref[...] = own_ref[pl.ds(at, quarter), :]
    near = jnp.concatenate([ref[...] for ref in rest[:-4]], axis=0)
    cut = first_ref.shape[0]
    first_ref[...] = near[:cut]
    second_ref[...] = near[cut:]


def spread_terms(dest, dest_inverse, block, far, counts):
    products = lax.dot_general(
        dest, block, (((1,), (1,)), ((), ())), preferred_element_type=jnp.float32
    )
    cosine = products * dest_inverse * far
    halfway = (1.0 + cosine) * 0.5
    weight = halfway * halfway * halfway
    coefficient = (weight * far).astype(jnp.bfloat16).astype(jnp.float32)
    spread = coefficient * counts.astype(jnp.float32)
    high = spread.astype(jnp.bfloat16)
    low = (spread - high.astype(jnp.float32)).astype(jnp.bfloat16)
    return jnp.dot(high, block, preferred_element_type=jnp.float32) + jnp.dot(
        low, block, preferred_element_type=jnp.float32
    )


def early_kernel(queries_ref, twin_ref, own_ref, counts_ref, *rest):
    out_ref, held_ref, sem = rest[-3:]
    queries = fetch_queries(queries_ref, held_ref, 1, sem)
    queries.start()
    rows = own_ref.shape[0]
    block = jnp.concatenate([own_ref[...]] + [ref[...] for ref in rest[:-3]], axis=0)
    far = as_row(column_inverse(block.astype(jnp.float32)))
    for number, dest_ref in enumerate((twin_ref, own_ref)):
        lines = slice(number * rows, (number + 1) * rows)
        dest = dest_ref[...]
        values = dest.astype(jnp.float32)
        dest_inverse = column_inverse(values)
        terms = spread_terms(dest, dest_inverse, block, far, counts_ref[lines, : block.shape[0]])
        if number == 1:
            terms = terms + values * dest_inverse
        out_ref[lines, :] = terms
    queries.wait()


def middle_kernel(twin_ref, own_ref, early_ref, counts_ref, beside_ref, behind_ref, out_ref):
    rows = own_ref.shape[0]
    block = jnp.concatenate([beside_ref[...], behind_ref[...]], axis=0)
    far = as_row(column_inverse(block.astype(jnp.float32)))
    for number, dest_ref in enumerate((twin_ref, own_ref)):
        lines = slice(number * rows, (number + 1) * rows)
        dest = dest_ref[...]
        dest_inverse = column_inverse(dest.astype(jnp.float32))
        terms = spread_terms(dest, dest_inverse, block, far, counts_ref[lines, : block.shape[0]])
        out_ref[lines, :] = early_ref[lines, :] + terms


def late_kernel(number, dest_ref, early_ref, counts_ref, *rest):
    out_ref = rest[-1]
    rows = dest_ref.shape[0]
    lines = slice(number * rows, (number + 1) * rows)
    block = jnp.concatenate([ref[...] for ref in rest[:-1]], axis=0)
    far = as_row(column_inverse(block.astype(jnp.float32)))
    dest = dest_ref[...]
    dest_inverse = column_inverse(dest.astype(jnp.float32))
    terms = spread_terms(dest, dest_inverse, block, far, counts_ref[lines, : block.shape[0]])
    out_ref[...] = early_ref[lines, :] + terms


def score_kernel(own_a_ref, own_b_ref, twin_a_ref, twin_b_ref, first_ref, second_ref, augmented_ref, best_ref, rows_ref):
    rows = own_a_ref.shape[0]
    for number, (a_ref, b_ref) in enumerate(((own_a_ref, own_b_ref), (twin_a_ref, twin_b_ref))):
        summed = a_ref[...] + b_ref[...]
        augmented = (summed * column_inverse(summed)).astype(jnp.bfloat16)
        if number == 0:
            augmented_ref[...] = augmented
        rows_ref[number * rows : (number + 1) * rows, :] = augmented

    height = first_ref.shape[0]
    step = min(1024, height)
    tile = min(2048, height)
    for number, held_ref in enumerate((first_ref, second_ref)):

        @pl.loop(0, height // tile)
        def _(i):
            at = pl.multiple_of(i * tile, tile)
            line = pl.multiple_of(number * (height // 128) + i * (tile // 128), tile // 128)
            found = []
            for first in range(0, tile, step):
                scores = lax.dot_general(
                    rows_ref[...],
                    held_ref[pl.ds(at + first, step), :],
                    (((1,), (1,)), ((), ())),
                    preferred_element_type=jnp.float32,
                )
                best = jnp.max(scores, axis=0, keepdims=True)
                found += [best[:, part : part + 128] for part in range(0, step, 128)]
            best_ref[pl.ds(line, tile // 128), :] = jnp.concatenate(found, axis=0)


def local(database, neighbours, valid_count, queries):
    rows, features = database.shape
    fanout = neighbours.shape[1]
    count = queries.shape[0]
    owners = lax.axis_size("db")
    panels = lax.axis_size("pb")
    assert panels == 4 and owners % 4 == 0 and owners & (owners - 1) == 0
    planes = owners // 2
    quarter = rows // panels
    me = lax.axis_index("pb")
    core = lax.axis_index("db") % 2

    def along(value, even, odd):
        apart = (even, odd)
        pairs = [(i, ((i // 2) ^ apart[i % 2]) * 2 + i % 2) for i in range(owners)]
        return lax.ppermute(value, "db", pairs)

    def swap(value):
        return lax.ppermute(value, "db", [(i, i ^ 1) for i in range(owners)])

    def cross(value, bits):
        pairs = []
        for panel in range(panels):
            for i in range(owners):
                pairs.append((panel * owners + i, (panel ^ bits[i % 2]) * owners + i))
        return lax.ppermute(value, ("pb", "db"), pairs)

    mine = lax.dynamic_slice_in_dim(database, me * quarter, quarter, 0)
    pieces = [along(mine, apart, apart) for apart in range(1, planes)]
    twin = swap(database)
    vmem = pl.BlockSpec(memory_space=pltpu.VMEM)
    slots = jnp.arange(fanout, dtype=jnp.int32)[None, :]
    wanted = jnp.where(slots < valid_count[:, None], neighbours, -1).reshape(-1, 128)
    twin_wanted = swap(wanted)
    padded = lambda size: (size + 127) // 128 * 128
    span = (planes - 1) * quarter
    early_counts, middle_counts, late_counts, own, first_queries = pl.pallas_call(
        functools.partial(count_kernel, planes),
        out_shape=[
            jax.ShapeDtypeStruct((2 * rows, padded(rows + span)), jnp.bfloat16),
            jax.ShapeDtypeStruct((2 * rows, padded(span)), jnp.bfloat16),
            jax.ShapeDtypeStruct((2 * rows, padded(2 * span)), jnp.bfloat16),
            jax.ShapeDtypeStruct((rows, features), jnp.bfloat16),
            jax.ShapeDtypeStruct((count // 4, features), jnp.bfloat16),
        ],
        in_specs=[vmem, vmem] + [pl.BlockSpec(memory_space=pltpu.HBM)] * 2,
        out_specs=[vmem] * 5,
        scratch_shapes=[
            pltpu.VMEM((2 * wanted.shape[0], 128), jnp.int32),
            pltpu.VMEM((2 * wanted.shape[0], 128), jnp.int32),
            pltpu.SemaphoreType.DMA(()),
            pltpu.SemaphoreType.DMA(()),
        ],
        compiler_params=pltpu.CompilerParams(vmem_limit_bytes=30 * MIB),
        cost_estimate=pl.CostEstimate(flops=1 << 26, bytes_accessed=4 * rows * rows, transcendentals=0),
        name="counts",
    )(twin_wanted, wanted, database, queries)
    piece = lambda height: jax.ShapeDtypeStruct((height, features), jnp.bfloat16)
    both, alone, *near = pl.pallas_call(
        join_kernel,
        out_shape=[piece(2 * quarter), piece(quarter), piece(span // 2), piece(span // 2)],
        in_specs=[vmem] * (2 + len(pieces)),
        out_specs=[vmem] * 4,
        compiler_params=pltpu.CompilerParams(vmem_limit_bytes=8 * MIB),
        name="join",
    )(own, twin, *pieces)
    across = [along(alone, 1, 1)] + [along(both, apart, apart + 1) for apart in range(2, planes, 2)]
    beside = [cross(part, (1, 2)) for part in near]
    behind = [cross(part, (2, 1)) for part in near]

    early, second_queries = pl.pallas_call(
        early_kernel,
        out_shape=[
            jax.ShapeDtypeStruct((2 * rows, features), jnp.float32),
            jax.ShapeDtypeStruct((count // 4, features), jnp.bfloat16),
        ],
        in_specs=[pl.BlockSpec(memory_space=pltpu.HBM)] + [vmem] * 5,
        out_specs=[vmem] * 2,
        scratch_shapes=[pltpu.SemaphoreType.DMA(())],
        compiler_params=pltpu.CompilerParams(vmem_limit_bytes=30 * MIB),
        cost_estimate=pl.CostEstimate(flops=1 << 26, bytes_accessed=4 * rows * rows, transcendentals=0),
        name="early_sums",
    )(queries, twin, own, early_counts, *near)

    middle = pl.pallas_call(
        middle_kernel,
        out_shape=jax.ShapeDtypeStruct((2 * rows, features), jnp.float32),
        in_specs=[vmem] * 6,
        out_specs=vmem,
        compiler_params=pltpu.CompilerParams(vmem_limit_bytes=30 * MIB),
        cost_estimate=pl.CostEstimate(flops=1 << 26, bytes_accessed=4 * rows * rows, transcendentals=0),
        name="middle_sums",
    )(twin, own, early, middle_counts, beside[0], behind[0])

    def late(number, dest):
        return pl.pallas_call(
            functools.partial(late_kernel, number),
            out_shape=jax.ShapeDtypeStruct((rows, features), jnp.float32),
            in_specs=[vmem] * (5 + len(across)),
            out_specs=vmem,
            compiler_params=pltpu.CompilerParams(vmem_limit_bytes=30 * MIB),
            name="late_sums",
        )(dest, middle, late_counts, *across, beside[1], behind[1])

    twin_a = late(0, twin)
    own_b = swap(twin_a)
    own_a = late(1, own)
    twin_b = swap(own_a)

    half = count // 2
    augmented, best = pl.pallas_call(
        score_kernel,
        out_shape=[
            jax.ShapeDtypeStruct((rows, features), jnp.bfloat16),
            jax.ShapeDtypeStruct((half // 128, 128), jnp.float32),
        ],
        in_specs=[vmem] * 6,
        out_specs=[vmem, vmem],
        scratch_shapes=[pltpu.VMEM((2 * rows, features), jnp.bfloat16)],
        compiler_params=pltpu.CompilerParams(vmem_limit_bytes=30 * MIB),
        cost_estimate=pl.CostEstimate(
            flops=2 * count * rows * features, bytes_accessed=count * features, transcendentals=0
        ),
        name="scores",
    )(own_a, own_b, twin_a, twin_b, first_queries, second_queries)

    apart = 1
    while apart < planes:
        best = jnp.maximum(best, along(best, apart, apart))
        apart *= 2
    other_half = swap(best)
    first = jnp.where(core == 0, best, other_half)
    second = jnp.where(core == 0, other_half, best)
    return augmented, jnp.concatenate([first, second], axis=0).reshape(count)


def solution(mesh):
    return jax.shard_map(
        local,
        mesh=mesh,
        in_specs=(P("db", None), P("db", None), P("db"), P("pb", None)),
        out_specs=(P("db", None), P("pb")),
        check_vma=False,
    )
```

profile of v0, /device:TPU:0, one launch (start us, length us, event | category | flops | bytes accessed | tf_op | source)
XLA Modules:
  0.0 51.5 jit_solution(1994328652914588285)
XLA Ops:
  0.6 0.5 %collective-permute-start.1 = (bf16[256,768]{1,0:T(8,128)(2,1)}, bf16[256,768]{1,0:T(8,128)(2,1)S(1)}, u32[]{:S(2)}, u32[]{:S(2)}) collective-permute-start(bf16[256,768]{1,0:T(8,128)(2,1)} %database_ref.1), channel_id=1, source_target_pairs={{0,1},{1,0},{2,3},{3,2},{4,5},{5,4},{6,7},{7,6},{8,9},{9,8},{10,11... | collective-permute-start | bytes 1179656 | tf_op jit(solution)/shard_map/ppermute | solution.py:235
  1.1 0.9 %constant_dynamic-slice_fusion = bf16[64,768]{1,0:T(8,128)(2,1)S(1)} fusion(bf16[256,768]{1,0:T(8,128)(2,1)} %database_ref.1, s32[]{:T(128)S(6)} %select_n.27), kind=kLoop, calls=%fused_computation.5 | loop fusion | bytes 196612 | tf_op jit(solution)/shard_map/dynamic_slice | solution.py:244
  2.0 2.6 %collective-permute-start.2 = (bf16[64,768]{1,0:T(8,128)(2,1)S(1)}, bf16[64,768]{1,0:T(8,128)(2,1)S(1)}, u32[]{:S(2)}, u32[]{:S(2)}) collective-permute-start(bf16[64,768]{1,0:T(8,128)(2,1)S(1)} %constant_dynamic-slice_fusion), channel_id=1, source_target_pairs={{0,2},{1,3},{2,0},{3,1},{4,6},{5,7},{6,4},{7,5},{8,10},{9,11},{10,... | collective-permute-start | bytes 294920 | tf_op jit(solution)/shard_map/ppermute | solution.py:232
  4.6 2.6 %collective-permute-start.3 = (bf16[64,768]{1,0:T(8,128)(2,1)S(1)}, bf16[64,768]{1,0:T(8,128)(2,1)S(1)}, u32[]{:S(2)}, u32[]{:S(2)}) collective-permute-start(bf16[64,768]{1,0:T(8,128)(2,1)S(1)} %constant_dynamic-slice_fusion), channel_id=1, source_target_pairs={{0,4},{1,5},{2,6},{3,7},{4,0},{5,1},{6,2},{7,3},{8,12},{9,13},{10,... | collective-permute-start | bytes 294920 | tf_op jit(solution)/shard_map/ppermute | solution.py:232
  7.2 0.7 %fusion = s32[256,16]{0,1:T(8,128)S(1)} fusion(s32[256,16]{0,1:T(8,128)} %param.5, s32[256]{0:T(256)} %param.6), kind=kLoop, calls=%fused_computation.2 | loop fusion | flops 8192 | bytes 33792 | tf_op jit(solution)/shard_map/jit(_where)/select_n | solution.py:249
  8.0 0.1 copy.7
  8.3 1.2 %collective-permute-done.twin_ref = s32[32,128]{1,0:T(8,128)S(1)} collective-permute-done((s32[32,128]{1,0:T(8,128)S(1)}, s32[32,128]{1,0:T(8,128)S(1)}, u32[]{:S(2)}, u32[]{:S(2)}) %collective-permute-start) | collective-permute-done | bytes 16416 | tf_op jit(solution)/shard_map/ppermute | solution.py:235
  9.4 1.0 %copy-done = bf16[256,768]{1,0:T(8,128)(2,1)S(1)} copy-done((bf16[256,768]{1,0:T(8,128)(2,1)S(1)}, bf16[256,768]{1,0:T(8,128)(2,1)}, u32[]{:S(2)}) %copy-start) | copy-done | bytes 393240
  10.4 3.0 %counts.1 = (bf16[512,512]{1,0:T(8,128)(2,1)S(1)}, bf16[512,256]{1,0:T(8,128)(2,1)S(1)}, bf16[512,384]{1,0:T(8,128)(2,1)S(1)}, bf16[256,768]{1,0:T(8,128)(2,1)S(1)}, bf16[4096,768]{1,0:T(8,128)(2,1)S(1)}) custom-call(s32[32,128]{1,0:T(8,128)S(1)} %collective-permute-done.twin_ref, s32[32,128]{1,0:T(8,128)S(1)} %reshape.11.own_ref, ...), custom_call_target="tpu_custom_call" | custom-call | flops 67108864 | bytes 262144 | tf_op jit(solution)/shard_map/counts/pallas_call | solution.py:253
  13.4 2.0 %collective-permute-done.3.rest_1_ = bf16[64,768]{1,0:T(8,128)(2,1)S(1)} collective-permute-done((bf16[64,768]{1,0:T(8,128)(2,1)S(1)}, bf16[64,768]{1,0:T(8,128)(2,1)S(1)}, u32[]{:S(2)}, u32[]{:S(2)}) %collective-permute-start.3) | collective-permute-done | bytes 98336 | tf_op jit(solution)/shard_map/ppermute | solution.py:232
  15.4 1.6 %collective-permute-start.5 = (bf16[96,768]{1,0:T(8,128)(2,1)S(1)}, bf16[96,768]{1,0:T(8,128)(2,1)S(1)}, u32[]{:S(2)}, u32[]{:S(2)}) collective-permute-start(bf16[96,768]{1,0:T(8,128)(2,1)S(1)} %get-tuple-element.17.rest_0_), channel_id=1, source_target_pairs={{0,8},{1,17},{2,10},{3,19},{4,12},{5,21},{6,14},{7,23},{8,0},{9,25... | collective-permute-start | bytes 442376 | tf_op jit(solution)/shard_map/ppermute | solution.py:242
  17.0 3.0 %collective-permute-start.8 = (bf16[128,768]{1,0:T(8,128)(2,1)S(1)}, bf16[128,768]{1,0:T(8,128)(2,1)S(1)}, u32[]{:S(2)}, u32[]{:S(2)}) collective-permute-start(bf16[128,768]{1,0:T(8,128)(2,1)S(1)} %get-tuple-element.23), channel_id=1, source_target_pairs={{0,4},{1,7},{2,6},{3,5},{4,0},{5,3},{6,2},{7,1},{8,12},{9,15},{10,... | collective-permute-start | bytes 589832 | tf_op jit(solution)/shard_map/ppermute | solution.py:232
  20.0 1.5 %collective-permute-start.6 = (bf16[96,768]{1,0:T(8,128)(2,1)S(1)}, bf16[96,768]{1,0:T(8,128)(2,1)S(1)}, u32[]{:S(2)}, u32[]{:S(2)}) collective-permute-start(bf16[96,768]{1,0:T(8,128)(2,1)S(1)} %get-tuple-element.17.rest_0_), channel_id=1, source_target_pairs={{0,16},{1,9},{2,18},{3,11},{4,20},{5,13},{6,22},{7,15},{8,24},{9,1... | collective-permute-start | bytes 442376 | tf_op jit(solution)/shard_map/ppermute | solution.py:242
  21.5 0.5 collective-permute-start.10
  22.0 0.5 %collective-permute-start.9 = (bf16[96,768]{1,0:T(8,128)(2,1)S(1)}, bf16[96,768]{1,0:T(8,128)(2,1)S(1)}, u32[]{:S(2)}, u32[]{:S(2)}) collective-permute-start(bf16[96,768]{1,0:T(8,128)(2,1)S(1)} %get-tuple-element.18.rest_1_), channel_id=1, source_target_pairs={{0,8},{1,17},{2,10},{3,19},{4,12},{5,21},{6,14},{7,23},{8,0},{9,25... | collective-permute-start | bytes 442376 | tf_op jit(solution)/shard_map/ppermute | solution.py:242
  22.6 0.6 %collective-permute-start.7 = (bf16[64,768]{1,0:T(8,128)(2,1)S(1)}, bf16[64,768]{1,0:T(8,128)(2,1)S(1)}, u32[]{:S(2)}, u32[]{:S(2)}) collective-permute-start(bf16[64,768]{1,0:T(8,128)(2,1)S(1)} %get-tuple-element.22), channel_id=1, source_target_pairs={{0,2},{1,3},{2,0},{3,1},{4,6},{5,7},{6,4},{7,5},{8,10},{9,11},{10,... | collective-permute-start | bytes 294920 | tf_op jit(solution)/shard_map/ppermute | solution.py:232
  23.2 2.8 %early_sums.1 = (f32[512,768]{1,0:T(8,128)S(1)}, bf16[4096,768]{1,0:T(8,128)(2,1)S(1)}) custom-call(bf16[16384,768]{1,0:T(8,128)(2,1)} %queries_ref.3, bf16[256,768]{1,0:T(8,128)(2,1)S(1)} %collective-permute-done.1.twin_ref.dest_ref, bf16[256,768]{1,0:T(8,128)(2,1)S(1)} %get-tuple-element.15.own_ref.dest_ref, ...), custom_call_target="tpu_custom_call" | custom-call | flops 67108864 | bytes 262144 | tf_op jit(solution)/shard_map/early_sums/pallas_call | solution.py:287
  26.0 1.1 %middle_sums.1.early_ref = f32[512,768]{1,0:T(8,128)S(1)} custom-call(bf16[256,768]{1,0:T(8,128)(2,1)S(1)} %collective-permute-done.1.twin_ref.dest_ref, bf16[256,768]{1,0:T(8,128)(2,1)S(1)} %get-tuple-element.15.own_ref.dest_ref, f32[512,768]{1,0:T(8,128)S(1)} %get-tuple-element.19.early_ref, bf16[512,256]{1,0:T(8,128)(2,1)S(1)} %get-tuple-element.20.counts_ref, ...), custom_call_target="tpu_custom_call" | custom-call | flops 67108864 | bytes 262144 | tf_op jit(solution)/shard_map/middle_sums/pallas_call | solution.py:301
  27.1 1.1 %collective-permute-done.7.rest_0_ = bf16[64,768]{1,0:T(8,128)(2,1)S(1)} collective-permute-done((bf16[64,768]{1,0:T(8,128)(2,1)S(1)}, bf16[64,768]{1,0:T(8,128)(2,1)S(1)}, u32[]{:S(2)}, u32[]{:S(2)}) %collective-permute-start.7) | collective-permute-done | bytes 98336 | tf_op jit(solution)/shard_map/ppermute | solution.py:232
  28.2 0.2 collective-permute-done.8.rest_1_
  28.4 1.1 %late_sums.3.twin_a_ref = f32[256,768]{1,0:T(8,128)S(1)} custom-call(bf16[256,768]{1,0:T(8,128)(2,1)S(1)} %collective-permute-done.1.twin_ref.dest_ref, f32[512,768]{1,0:T(8,128)S(1)} %middle_sums.1.early_ref, bf16[512,384]{1,0:T(8,128)(2,1)S(1)} %get-tuple-element.21.counts_ref, bf16[64,768]{1,0:T(8,128)(2,1)S(1)} %collective-permute-done.7.rest_0_, ...), custom_call_target="tpu_custom_call" | custom-call | tf_op jit(solution)/shard_map/late_sums/pallas_call | solution.py:312
  29.6 1.1 %late_sums.2.own_a_ref = f32[256,768]{1,0:T(8,128)S(1)} custom-call(bf16[256,768]{1,0:T(8,128)(2,1)S(1)} %get-tuple-element.15.own_ref.dest_ref, f32[512,768]{1,0:T(8,128)S(1)} %middle_sums.1.early_ref, bf16[512,384]{1,0:T(8,128)(2,1)S(1)} %get-tuple-element.21.counts_ref, bf16[64,768]{1,0:T(8,128)(2,1)S(1)} %collective-permute-done.7.rest_0_, ...), custom_call_target="tpu_custom_call" | custom-call | tf_op jit(solution)/shard_map/late_sums/pallas_call | solution.py:312
  30.6 0.6 %collective-permute-start.12 = (f32[256,768]{1,0:T(8,128)S(1)}, f32[256,768]{1,0:T(8,128)S(1)}, u32[]{:S(2)}, u32[]{:S(2)}) collective-permute-start(f32[256,768]{1,0:T(8,128)S(1)} %late_sums.2.own_a_ref), channel_id=1, source_target_pairs={{0,1},{1,0},{2,3},{3,2},{4,5},{5,4},{6,7},{7,6},{8,9},{9,8},{10,11... | collective-permute-start | bytes 2359304 | tf_op jit(solution)/shard_map/ppermute | solution.py:235
  31.2 0.6 %collective-permute-done.11.own_b_ref = f32[256,768]{1,0:T(8,128)S(1)} collective-permute-done((f32[256,768]{1,0:T(8,128)S(1)}, f32[256,768]{1,0:T(8,128)S(1)}, u32[]{:S(2)}, u32[]{:S(2)}) %collective-permute-start.11) | collective-permute-done | bytes 786464 | tf_op jit(solution)/shard_map/ppermute | solution.py:235
  31.8 1.3 %collective-permute-done.12.twin_b_ref = f32[256,768]{1,0:T(8,128)S(1)} collective-permute-done((f32[256,768]{1,0:T(8,128)S(1)}, f32[256,768]{1,0:T(8,128)S(1)}, u32[]{:S(2)}, u32[]{:S(2)}) %collective-permute-start.12) | collective-permute-done | bytes 786464 | tf_op jit(solution)/shard_map/ppermute | solution.py:235
  33.1 7.6 %scores.1 = (bf16[256,768]{1,0:T(8,128)(2,1)}, f32[64,128]{1,0:T(8,128)S(1)}) custom-call(f32[256,768]{1,0:T(8,128)S(1)} %late_sums.2.own_a_ref, f32[256,768]{1,0:T(8,128)S(1)} %collective-permute-done.11.own_b_ref, f32[256,768]{1,0:T(8,128)S(1)} %late_sums.3.twin_a_ref, f32[256,768]{1,0:T(8,128)S(1)} %collective-permute-done.12.twin_b_ref, ...), custom_call_target="tpu_custom_call" | custom-call | flops 6442450944 | bytes 12582912 | tf_op jit(solution)/shard_map/scores/pallas_call | solution.py:327
  40.7 0.3 collective-permute-start.13
  41.0 3.7 %collective-permute-done.13 = f32[64,128]{1,0:T(8,128)S(1)} collective-permute-done((f32[64,128]{1,0:T(8,128)S(1)}, f32[64,128]{1,0:T(8,128)S(1)}, u32[]{:S(2)}, u32[]{:S(2)}) %collective-permute-start.13) | collective-permute-done | bytes 32800 | tf_op jit(solution)/shard_map/ppermute | solution.py:232
  44.7 1.5 %collective-permute-start.14 = (f32[64,128]{1,0:T(8,128)S(1)}, f32[64,128]{1,0:T(8,128)S(1)}, u32[]{:S(2)}, u32[]{:S(2)}) collective-permute-start(f32[64,128]{1,0:T(8,128)S(1)} %max.6), channel_id=1, source_target_pairs={{0,4},{1,5},{2,6},{3,7},{4,0},{5,1},{6,2},{7,3},{8,12},{9,13},{10,... | collective-permute-start | bytes 98312 | tf_op jit(solution)/shard_map/ppermute | solution.py:232
  46.2 3.4 %collective-permute-done.14 = f32[64,128]{1,0:T(8,128)S(1)} collective-permute-done((f32[64,128]{1,0:T(8,128)S(1)}, f32[64,128]{1,0:T(8,128)S(1)}, u32[]{:S(2)}, u32[]{:S(2)}) %collective-permute-start.14) | collective-permute-done | bytes 32800 | tf_op jit(solution)/shard_map/ppermute | solution.py:232
  49.6 1.2 %collective-permute-done.15 = f32[64,128]{1,0:T(8,128)S(1)} collective-permute-done((f32[64,128]{1,0:T(8,128)S(1)}, f32[64,128]{1,0:T(8,128)S(1)}, u32[]{:S(2)}, u32[]{:S(2)}) %collective-permute-start.15) | collective-permute-done | bytes 32800 | tf_op jit(solution)/shard_map/ppermute | solution.py:235
  50.8 0.6 %maximum_bitcast_fusion = f32[16384]{0:T(1024)} fusion(f32[64,128]{1,0:T(8,128)S(1)} %get-tuple-element.29, f32[64,128]{1,0:T(8,128)S(1)} %get-tuple-element.28), kind=kLoop, calls=%fused_computation | loop fusion | flops 16384 | bytes 131072 | tf_op jit(solution)/shard_map/reshape | solution.py:350
  (17 shorter events, 0.3 us)
Async XLA Ops:
  0.6 14.8 %collective-permute-start.1 = (bf16[256,768]{1,0:T(8,128)(2,1)}, bf16[256,768]{1,0:T(8,128)(2,1)S(1)}, u32[]{:S(2)}, u32[]{:S(2)}) collective-permute-start(bf16[256,768]{1,0:T(8,128)(2,1)} %database_ref.1), channel_id=1, source_target_pairs={{0,1},{1,0},{2,3},{3,2},{4,5},{5,4},{6,7},{7,6},{8,9},{9,8},{10,11... | collective-permute-start | bytes 1179656 | tf_op jit(solution)/shard_map/ppermute | solution.py:235
  2.0 11.4 %collective-permute-start.2 = (bf16[64,768]{1,0:T(8,128)(2,1)S(1)}, bf16[64,768]{1,0:T(8,128)(2,1)S(1)}, u32[]{:S(2)}, u32[]{:S(2)}) collective-permute-start(bf16[64,768]{1,0:T(8,128)(2,1)S(1)} %constant_dynamic-slice_fusion), channel_id=1, source_target_pairs={{0,2},{1,3},{2,0},{3,1},{4,6},{5,7},{6,4},{7,5},{8,10},{9,11},{10,... | collective-permute-start | bytes 294920 | tf_op jit(solution)/shard_map/ppermute | solution.py:232
  4.6 10.7 %collective-permute-start.3 = (bf16[64,768]{1,0:T(8,128)(2,1)S(1)}, bf16[64,768]{1,0:T(8,128)(2,1)S(1)}, u32[]{:S(2)}, u32[]{:S(2)}) collective-permute-start(bf16[64,768]{1,0:T(8,128)(2,1)S(1)} %constant_dynamic-slice_fusion), channel_id=1, source_target_pairs={{0,4},{1,5},{2,6},{3,7},{4,0},{5,1},{6,2},{7,3},{8,12},{9,13},{10,... | collective-permute-start | bytes 294920 | tf_op jit(solution)/shard_map/ppermute | solution.py:232
  7.2 8.2 %collective-permute-start.4 = (bf16[64,768]{1,0:T(8,128)(2,1)S(1)}, bf16[64,768]{1,0:T(8,128)(2,1)S(1)}, u32[]{:S(2)}, u32[]{:S(2)}) collective-permute-start(bf16[64,768]{1,0:T(8,128)(2,1)S(1)} %constant_dynamic-slice_fusion), channel_id=1, source_target_pairs={{0,6},{1,7},{2,4},{3,5},{4,2},{5,3},{6,0},{7,1},{8,14},{9,15},{10,... | collective-permute-start | bytes 294920 | tf_op jit(solution)/shard_map/ppermute | solution.py:232
  8.2 1.2 %collective-permute-start = (s32[32,128]{1,0:T(8,128)S(1)}, s32[32,128]{1,0:T(8,128)S(1)}, u32[]{:S(2)}, u32[]{:S(2)}) collective-permute-start(s32[32,128]{1,0:T(8,128)S(1)} %reshape.11.own_ref), channel_id=1, source_target_pairs={{0,1},{1,0},{2,3},{3,2},{4,5},{5,4},{6,7},{7,6},{8,9},{9,8},{10,11... | collective-permute-start | bytes 49160 | tf_op jit(solution)/shard_map/ppermute | solution.py:235
  9.4 1.0 %copy-start = (bf16[256,768]{1,0:T(8,128)(2,1)S(1)}, bf16[256,768]{1,0:T(8,128)(2,1)}, u32[]{:S(2)}) copy-start(bf16[256,768]{1,0:T(8,128)(2,1)} %database_ref.1) | copy-start | bytes 1179652
  15.4 7.1 %collective-permute-start.5 = (bf16[96,768]{1,0:T(8,128)(2,1)S(1)}, bf16[96,768]{1,0:T(8,128)(2,1)S(1)}, u32[]{:S(2)}, u32[]{:S(2)}) collective-permute-start(bf16[96,768]{1,0:T(8,128)(2,1)S(1)} %get-tuple-element.17.rest_0_), channel_id=1, source_target_pairs={{0,8},{1,17},{2,10},{3,19},{4,12},{5,21},{6,14},{7,23},{8,0},{9,25... | collective-permute-start | bytes 442376 | tf_op jit(solution)/shard_map/ppermute | solution.py:242
  17.0 11.4 %collective-permute-start.8 = (bf16[128,768]{1,0:T(8,128)(2,1)S(1)}, bf16[128,768]{1,0:T(8,128)(2,1)S(1)}, u32[]{:S(2)}, u32[]{:S(2)}) collective-permute-start(bf16[128,768]{1,0:T(8,128)(2,1)S(1)} %get-tuple-element.23), channel_id=1, source_target_pairs={{0,4},{1,7},{2,6},{3,5},{4,0},{5,3},{6,2},{7,1},{8,12},{9,15},{10,... | collective-permute-start | bytes 589832 | tf_op jit(solution)/shard_map/ppermute | solution.py:232
  20.0 6.0 %collective-permute-start.6 = (bf16[96,768]{1,0:T(8,128)(2,1)S(1)}, bf16[96,768]{1,0:T(8,128)(2,1)S(1)}, u32[]{:S(2)}, u32[]{:S(2)}) collective-permute-start(bf16[96,768]{1,0:T(8,128)(2,1)S(1)} %get-tuple-element.17.rest_0_), channel_id=1, source_target_pairs={{0,16},{1,9},{2,18},{3,11},{4,20},{5,13},{6,22},{7,15},{8,24},{9,1... | collective-permute-start | bytes 442376 | tf_op jit(solution)/shard_map/ppermute | solution.py:242
  21.5 6.7 %collective-permute-start.10 = (bf16[96,768]{1,0:T(8,128)(2,1)S(1)}, bf16[96,768]{1,0:T(8,128)(2,1)S(1)}, u32[]{:S(2)}, u32[]{:S(2)}) collective-permute-start(bf16[96,768]{1,0:T(8,128)(2,1)S(1)} %get-tuple-element.18.rest_1_), channel_id=1, source_target_pairs={{0,16},{1,9},{2,18},{3,11},{4,20},{5,13},{6,22},{7,15},{8,24},{9,1... | collective-permute-start | bytes 442376 | tf_op jit(solution)/shard_map/ppermute | solution.py:242
  22.0 6.2 %collective-permute-start.9 = (bf16[96,768]{1,0:T(8,128)(2,1)S(1)}, bf16[96,768]{1,0:T(8,128)(2,1)S(1)}, u32[]{:S(2)}, u32[]{:S(2)}) collective-permute-start(bf16[96,768]{1,0:T(8,128)(2,1)S(1)} %get-tuple-element.18.rest_1_), channel_id=1, source_target_pairs={{0,8},{1,17},{2,10},{3,19},{4,12},{5,21},{6,14},{7,23},{8,0},{9,25... | collective-permute-start | bytes 442376 | tf_op jit(solution)/shard_map/ppermute | solution.py:242
  22.6 5.7 %collective-permute-start.7 = (bf16[64,768]{1,0:T(8,128)(2,1)S(1)}, bf16[64,768]{1,0:T(8,128)(2,1)S(1)}, u32[]{:S(2)}, u32[]{:S(2)}) collective-permute-start(bf16[64,768]{1,0:T(8,128)(2,1)S(1)} %get-tuple-element.22), channel_id=1, source_target_pairs={{0,2},{1,3},{2,0},{3,1},{4,6},{5,7},{6,4},{7,5},{8,10},{9,11},{10,... | collective-permute-start | bytes 294920 | tf_op jit(solution)/shard_map/ppermute | solution.py:232
  29.5 2.4 %collective-permute-start.11 = (f32[256,768]{1,0:T(8,128)S(1)}, f32[256,768]{1,0:T(8,128)S(1)}, u32[]{:S(2)}, u32[]{:S(2)}) collective-permute-start(f32[256,768]{1,0:T(8,128)S(1)} %late_sums.3.twin_a_ref), channel_id=1, source_target_pairs={{0,1},{1,0},{2,3},{3,2},{4,5},{5,4},{6,7},{7,6},{8,9},{9,8},{10,11... | collective-permute-start | bytes 2359304 | tf_op jit(solution)/shard_map/ppermute | solution.py:235
  30.6 2.5 %collective-permute-start.12 = (f32[256,768]{1,0:T(8,128)S(1)}, f32[256,768]{1,0:T(8,128)S(1)}, u32[]{:S(2)}, u32[]{:S(2)}) collective-permute-start(f32[256,768]{1,0:T(8,128)S(1)} %late_sums.2.own_a_ref), channel_id=1, source_target_pairs={{0,1},{1,0},{2,3},{3,2},{4,5},{5,4},{6,7},{7,6},{8,9},{9,8},{10,11... | collective-permute-start | bytes 2359304 | tf_op jit(solution)/shard_map/ppermute | solution.py:235
  40.7 4.0 %collective-permute-start.13 = (f32[64,128]{1,0:T(8,128)S(1)}, f32[64,128]{1,0:T(8,128)S(1)}, u32[]{:S(2)}, u32[]{:S(2)}) collective-permute-start(f32[64,128]{1,0:T(8,128)S(1)} %get-tuple-element.27), channel_id=1, source_target_pairs={{0,2},{1,3},{2,0},{3,1},{4,6},{5,7},{6,4},{7,5},{8,10},{9,11},{10,... | collective-permute-start | bytes 98312 | tf_op jit(solution)/shard_map/ppermute | solution.py:232
  44.7 4.9 %collective-permute-start.14 = (f32[64,128]{1,0:T(8,128)S(1)}, f32[64,128]{1,0:T(8,128)S(1)}, u32[]{:S(2)}, u32[]{:S(2)}) collective-permute-start(f32[64,128]{1,0:T(8,128)S(1)} %max.6), channel_id=1, source_target_pairs={{0,4},{1,5},{2,6},{3,7},{4,0},{5,1},{6,2},{7,3},{8,12},{9,13},{10,... | collective-permute-start | bytes 98312 | tf_op jit(solution)/shard_map/ppermute | solution.py:232
  49.6 1.2 %collective-permute-start.15 = (f32[64,128]{1,0:T(8,128)S(1)}, f32[64,128]{1,0:T(8,128)S(1)}, u32[]{:S(2)}, u32[]{:S(2)}) collective-permute-start(f32[64,128]{1,0:T(8,128)S(1)} %max.7), channel_id=1, source_target_pairs={{0,1},{1,0},{2,3},{3,2},{4,5},{5,4},{6,7},{7,6},{8,9},{9,8},{10,11... | collective-permute-start | bytes 98312 | tf_op jit(solution)/shard_map/ppermute | solution.py:235
where the time goes:
time: 51.8 us; the launch traced here: 51.5 us
  Pallas kernels  16.7 us (32%)
  starting transfers between devices  15.9 us (31%)
  waiting for transfers between devices  14.7 us (28%)
  local copies, waits for them, and re-layouts  2.1 us (4%)
  other arithmetic  1.38 us (3%)
  between operations  0.76 us (1%)
    ppermute x7, starting transfers between devices, along(): return lax.ppermute(value, 'db', pairs)  10.5 us
    ppermute x7, waiting for transfers between devices, along(): return lax.ppermute(value, 'db', pairs)  10.4 us
    pallas_call x1, Pallas kernels, local(): pl.pallas_call(score_kernel, out_shape=[jax.ShapeDtypeStruct((rows, featu...  7.61 us
    ppermute x5, waiting for transfers between devices, swap(): return lax.ppermute(value, 'db', [(i, i ^ 1) for i in range(owners)])  4.27 us
    ppermute x4, starting transfers between devices, cross(): return lax.ppermute(value, ('pb', 'db'), pairs)  4.12 us
    pallas_call x1, Pallas kernels, local(): pl.pallas_call(functools.partial(count_kernel, planes), out_shape=[jax.Sh...  3 us
    pallas_call x1, Pallas kernels, local(): pl.pallas_call(early_kernel, out_shape=[jax.ShapeDtypeStruct((2 * rows, f...  2.82 us
    pallas_call x2, Pallas kernels, late(): pl.pallas_call(functools.partial(late_kernel, number), out_shape=jax.Shap...  2.12 us
  transfers between devices with their start and end apart: 16, of which 9 were waited for; matrix products, arithmetic and copies ran while one was open for 4% of the time, Pallas kernels for 16%

commit v1 on v0

--- a/solution.py
+++ b/solution.py
@@ -28,22 +28,23 @@
 
 def fetch_queries(queries_ref, held_ref, part, sem):
     rows = held_ref.shape[0]
-    core = position_of()[2]
-    start = pl.multiple_of((core * 2 + part) * rows, rows)
+    half = queries_ref.shape[0] // 2
+    start = pl.multiple_of(position_of()[2] * half + part * rows, rows)
     return pltpu.make_async_copy(queries_ref.at[pl.ds(start, rows), :], held_ref, sem)
 
 
 def count_kernel(
-    planes, twin_ref, own_ref, database_ref, queries_ref, early_ref, middle_ref, late_ref, copy_ref, held_ref,
-    tiles_ref, lows_ref, sem, queries_sem,
+    planes, twin_ref, own_ref, database_ref, queries_ref, *rest
 ):
+    count_refs = rest[:-6]
+    copy_ref, held_ref, tiles_ref, lows_ref, sem, queries_sem = rest[-6:]
     rows = copy_ref.shape[0]
     fanout = own_ref.shape[0] * 128 // rows
     quarter = rows // 4
     span = (planes - 1) * quarter
-    early_tiles = early_ref.shape[1] // 128
-    middle_tiles = middle_ref.shape[1] // 128
-    late_tiles = late_ref.shape[1] // 128
+    starts = [0]
+    for count_ref in count_refs:
+        starts.append(starts[-1] + count_ref.shape[1])
     cut = span // 2
     copy = pltpu.make_async_copy(database_ref, copy_ref, sem)
     copy.start()
@@ -64,21 +65,19 @@
         held = jnp.where(paired, away & 1, side) == core
         straight = (away - 1) * quarter
         crossed = ((away >> 1) * 2 - 1 + (side ^ core)) * quarter
-        middle = early_tiles * 128
-        late = middle + middle_tiles * 128
         straight = straight + inner
         crossed = crossed + inner
         second = jnp.where(cross == 1 + core, 0, cut)
-        forwarded = straight + second + jnp.where(straight < cut, middle, late + span - cut)
-        position = jnp.where(cross == 3, late + jnp.where(paired, crossed, straight), forwarded)
-        position = jnp.where(cross == 0, rows + straight, position)
+        forwarded = straight + second + jnp.where(straight < cut, starts[2], starts[3] - cut)
+        position = jnp.where(cross == 3, starts[4] + jnp.where(paired, crossed, straight), forwarded)
+        position = jnp.where(cross == 0, starts[1] + straight, position)
         position = jnp.where(away == 0, row, position)
         position = jnp.where((wanted >= 0) & held, position, -1)
         tiles_ref[number * lines : (number + 1) * lines, :] = position >> 7
         lows_ref[number * lines : (number + 1) * lines, :] = position & 127
 
     group = 16
-    height = (early_tiles + middle_tiles + late_tiles) * group
+    height = starts[-1] // 128 * group
     width = group * fanout
     at_row = lax.broadcasted_iota(jnp.int32, (height, width), 0)
     at_lane = lax.broadcasted_iota(jnp.int32, (height, width), 1)
@@ -99,7 +98,7 @@
         ).astype(jnp.bfloat16)
         start = pl.ds(pl.multiple_of(at * group, group), group)
         tile = 0
-        for count_ref in (early_ref, middle_ref, late_ref):
+        for count_ref in count_refs:
             for t in range(count_ref.shape[1] // 128):
                 count_ref[start, t * 128 : (t + 1) * 128] = counts[tile * group : (tile + 1) * group, :]
                 tile += 1
@@ -110,7 +109,7 @@
     queries.wait()
 
 
-def join_kernel(own_ref, twin_ref, *rest):
+def join_kernel(own_ref, twin_ref, total_ref, *rest):
     both_ref, alone_ref, first_ref, second_ref = rest[-4:]
     quarter = alone_ref.shape[0]
     me = position_of()[0]
@@ -140,12 +139,15 @@
     )
 
 
-def early_kernel(queries_ref, twin_ref, own_ref, counts_ref, *rest):
-    out_ref, held_ref, sem = rest[-3:]
-    queries = fetch_queries(queries_ref, held_ref, 1, sem)
-    queries.start()
+def sums_kernel(blocks, part, twin_ref, own_ref, counts_ref, *rest):
+    block_refs, rest = rest[:blocks], rest[blocks:]
+    if part is not None:
+        queries_ref, *rest, held_ref, sem = rest
+        queries = fetch_queries(queries_ref, held_ref, part, sem)
+        queries.start()
+    *before_ref, out_ref = rest
     rows = own_ref.shape[0]
-    block = jnp.concatenate([own_ref[...]] + [ref[...] for ref in rest[:-3]], axis=0)
+    block = jnp.concatenate([ref[...] for ref in block_refs], axis=0) if blocks > 1 else block_refs[0][...]
     far = as_row(column_inverse(block.astype(jnp.float32)))
     for number, dest_ref in enumerate((twin_ref, own_ref)):
         lines = slice(number * rows, (number + 1) * rows)
@@ -153,22 +155,13 @@
         values = dest.astype(jnp.float32)
         dest_inverse = column_inverse(values)
         terms = spread_terms(dest, dest_inverse, block, far, counts_ref[lines, : block.shape[0]])
-        if number == 1:
+        if before_ref:
+            terms = before_ref[0][lines, :] + terms
+        elif number == 1:
             terms = terms + values * dest_inverse
         out_ref[lines, :] = terms
-    queries.wait()
-
-
-def middle_kernel(twin_ref, own_ref, early_ref, counts_ref, beside_ref, behind_ref, out_ref):
-    rows = own_ref.shape[0]
-    block = jnp.concatenate([beside_ref[...], behind_ref[...]], axis=0)
-    far = as_row(column_inverse(block.astype(jnp.float32)))
-    for number, dest_ref in enumerate((twin_ref, own_ref)):
-        lines = slice(number * rows, (number + 1) * rows)
-        dest = dest_ref[...]
-        dest_inverse = column_inverse(dest.astype(jnp.float32))
-        terms = spread_terms(dest, dest_inverse, block, far, counts_ref[lines, : block.shape[0]])
-        out_ref[lines, :] = early_ref[lines, :] + terms
+    if part is not None:
+        queries.wait()
 
 
 def late_kernel(number, dest_ref, early_ref, counts_ref, *rest):
@@ -183,7 +176,7 @@
     out_ref[...] = early_ref[lines, :] + terms
 
 
-def score_kernel(own_a_ref, own_b_ref, twin_a_ref, twin_b_ref, first_ref, second_ref, augmented_ref, best_ref, rows_ref):
+def score_kernel(own_a_ref, own_b_ref, twin_a_ref, twin_b_ref, first_ref, second_ref, third_ref, augmented_ref, best_ref, rows_ref):
     rows = own_a_ref.shape[0]
     for number, (a_ref, b_ref) in enumerate(((own_a_ref, own_b_ref), (twin_a_ref, twin_b_ref))):
         summed = a_ref[...] + b_ref[...]
@@ -192,15 +185,18 @@
             augmented_ref[...] = augmented
         rows_ref[number * rows : (number + 1) * rows, :] = augmented
 
-    height = first_ref.shape[0]
-    step = min(1024, height)
-    tile = min(2048, height)
-    for number, held_ref in enumerate((first_ref, second_ref)):
+    line_of = 0
+    for held_ref in (first_ref, second_ref, third_ref):
+        height = held_ref.shape[0]
+        step = min(1024, height)
+        tile = min(2048, height)
+        before = line_of
+        line_of += height // 128
 
         @pl.loop(0, height // tile)
         def _(i):
             at = pl.multiple_of(i * tile, tile)
-            line = pl.multiple_of(number * (height // 128) + i * (tile // 128), tile // 128)
+            line = pl.multiple_of(before + i * (tile // 128), tile // 128)
             found = []
             for first in range(0, tile, step):
                 scores = lax.dot_general(
@@ -250,17 +246,17 @@
     twin_wanted = swap(wanted)
     padded = lambda size: (size + 127) // 128 * 128
     span = (planes - 1) * quarter
-    early_counts, middle_counts, late_counts, own, first_queries = pl.pallas_call(
+    *counts, own, first_queries = pl.pallas_call(
         functools.partial(count_kernel, planes),
         out_shape=[
-            jax.ShapeDtypeStruct((2 * rows, padded(rows + span)), jnp.bfloat16),
-            jax.ShapeDtypeStruct((2 * rows, padded(span)), jnp.bfloat16),
-            jax.ShapeDtypeStruct((2 * rows, padded(2 * span)), jnp.bfloat16),
+            jax.ShapeDtypeStruct((2 * rows, padded(width)), jnp.bfloat16) for width in (rows,) + (span,) * 4
+        ]
+        + [
             jax.ShapeDtypeStruct((rows, features), jnp.bfloat16),
             jax.ShapeDtypeStruct((count // 4, features), jnp.bfloat16),
         ],
         in_specs=[vmem, vmem] + [pl.BlockSpec(memory_space=pltpu.HBM)] * 2,
-        out_specs=[vmem] * 5,
+        out_specs=[vmem] * 7,
         scratch_shapes=[
             pltpu.VMEM((2 * wanted.shape[0], 128), jnp.int32),
             pltpu.VMEM((2 * wanted.shape[0], 128), jnp.int32),
@@ -271,52 +267,58 @@
         cost_estimate=pl.CostEstimate(flops=1 << 26, bytes_accessed=4 * rows * rows, transcendentals=0),
         name="counts",
     )(twin_wanted, wanted, database, queries)
+
+    def sums(name, counts, blocks, before=None, part=None):
+        out = [jax.ShapeDtypeStruct((2 * rows, features), jnp.float32)]
+        operands = [twin, own, counts, *blocks]
+        specs = [vmem] * len(operands)
+        scratch = []
+        if part is not None:
+            operands.append(queries)
+            specs.append(pl.BlockSpec(memory_space=pltpu.HBM))
+            out.append(jax.ShapeDtypeStruct((count // 8, features), jnp.bfloat16))
+            scratch.append(pltpu.SemaphoreType.DMA(()))
+        if before is not None:
+            operands.append(before)
+            specs.append(vmem)
+        return pl.pallas_call(
+            functools.partial(sums_kernel, len(blocks), part),
+            out_shape=out,
+            in_specs=specs,
+            out_specs=[vmem] * len(out),
+            scratch_shapes=scratch,
+            compiler_params=pltpu.CompilerParams(vmem_limit_bytes=30 * MIB),
+            cost_estimate=pl.CostEstimate(flops=1 << 26, bytes_accessed=4 * rows * rows, transcendentals=0),
+            name=name,
+        )(*operands)
+
+    total, second_queries = sums("own_sums", counts[0], [own], part=2)
     piece = lambda height: jax.ShapeDtypeStruct((height, features), jnp.bfloat16)
     both, alone, *near = pl.pallas_call(
         join_kernel,
         out_shape=[piece(2 * quarter), piece(quarter), piece(span // 2), piece(span // 2)],
-        in_specs=[vmem] * (2 + len(pieces)),
+        in_specs=[vmem] * (3 + len(pieces)),
         out_specs=[vmem] * 4,
         compiler_params=pltpu.CompilerParams(vmem_limit_bytes=8 * MIB),
         name="join",
-    )(own, twin, *pieces)
+    )(own, twin, total, *pieces)
     across = [along(alone, 1, 1)] + [along(both, apart, apart + 1) for apart in range(2, planes, 2)]
     beside = [cross(part, (1, 2)) for part in near]
     behind = [cross(part, (2, 1)) for part in near]
 
-    early, second_queries = pl.pallas_call(
-        early_kernel,
-        out_shape=[
-            jax.ShapeDtypeStruct((2 * rows, features), jnp.float32),
-            jax.ShapeDtypeStruct((count // 4, features), jnp.bfloat16),
-        ],
-        in_specs=[pl.BlockSpec(memory_space=pltpu.HBM)] + [vmem] * 5,
-        out_specs=[vmem] * 2,
-        scratch_shapes=[pltpu.SemaphoreType.DMA(())],
-        compiler_params=pltpu.CompilerParams(vmem_limit_bytes=30 * MIB),
-        cost_estimate=pl.CostEstimate(flops=1 << 26, bytes_accessed=4 * rows * rows, transcendentals=0),
-        name="early_sums",
-    )(queries, twin, own, early_counts, *near)
-
-    middle = pl.pallas_call(
-        middle_kernel,
-        out_shape=jax.ShapeDtypeStruct((2 * rows, features), jnp.float32),
-        in_specs=[vmem] * 6,
-        out_specs=vmem,
-        compiler_params=pltpu.CompilerParams(vmem_limit_bytes=30 * MIB),
-        cost_estimate=pl.CostEstimate(flops=1 << 26, bytes_accessed=4 * rows * rows, transcendentals=0),
-        name="middle_sums",
-    )(twin, own, early, middle_counts, beside[0], behind[0])
+    total, third_queries = sums("near_sums", counts[1], near, total, part=3)
+    (total,) = sums("first_sums", counts[2], [beside[0], behind[0]], total)
+    (total,) = sums("second_sums", counts[3], [beside[1], behind[1]], total)
 
     def late(number, dest):
         return pl.pallas_call(
             functools.partial(late_kernel, number),
             out_shape=jax.ShapeDtypeStruct((rows, features), jnp.float32),
-            in_specs=[vmem] * (5 + len(across)),
+            in_specs=[vmem] * (3 + len(across)),
             out_specs=vmem,
             compiler_params=pltpu.CompilerParams(vmem_limit_bytes=30 * MIB),
             name="late_sums",
-        )(dest, middle, late_counts, *across, beside[1], behind[1])
+        )(dest, total, counts[4], *across)
 
     twin_a = late(0, twin)
     own_b = swap(twin_a)
@@ -330,7 +332,7 @@
             jax.ShapeDtypeStruct((rows, features), jnp.bfloat16),
             jax.ShapeDtypeStruct((half // 128, 128), jnp.float32),
         ],
-        in_specs=[vmem] * 6,
+        in_specs=[vmem] * 7,
         out_specs=[vmem, vmem],
         scratch_shapes=[pltpu.VMEM((2 * rows, features), jnp.bfloat16)],
         compiler_params=pltpu.CompilerParams(vmem_limit_bytes=30 * MIB),
@@ -338,12 +340,11 @@
             flops=2 * count * rows * features, bytes_accessed=count * features, transcendentals=0
         ),
         name="scores",
-    )(own_a, own_b, twin_a, twin_b, first_queries, second_queries)
-
-    apart = 1
-    while apart < planes:
-        best = jnp.maximum(best, along(best, apart, apart))
-        apart *= 2
+    )(own_a, own_b, twin_a, twin_b, first_queries, second_queries, third_queries)
+
+    received = [along(best, apart, apart) for apart in range(planes - 1, 0, -1)]
+    for value in received:
+        best = jnp.maximum(best, value)
     other_half = swap(best)
     first = jnp.where(core == 0, best, other_half)
     second = jnp.where(core == 0, other_half, best)

time: 51.8 us -> 51.9 us (level)
  waiting for transfers between devices: 14.7 us -> 7.95 us
  starting transfers between devices: 15.9 us -> 19.4 us
  Pallas kernels: 16.7 us -> 19.9 us
    ppermute x7 -> x8, waiting for transfers between devices: 10.4 us -> 3.57 us  [along(): return lax.ppermute(value, 'db', pairs)]
    pallas_call x2 -> x4, Pallas kernels: 3.93 us -> 7.49 us  [sums(): pl.pallas_call(functools.partial(sums_kernel, len(blocks), part), out_sha...]
    ppermute x7 -> x8, starting transfers between devices: 10.5 us -> 13.7 us  [along(): return lax.ppermute(value, 'db', pairs)]
  transfers between devices with their start and end apart: 16 -> 17, of which waited for: 9 -> 7; matrix products, arithmetic and copies ran while one was open for 4% -> 4% of each run, Pallas kernels for 16% -> 22%
where the time goes in v1:
time: 51.9 us; the launch traced here: 51.5 us
  Pallas kernels  19.9 us (38%)
  starting transfers between devices  19.4 us (37%)
  waiting for transfers between devices  7.95 us (15%)
  local copies, waits for them, and re-layouts  2.1 us (4%)
  other arithmetic  1.38 us (3%)
  between operations  0.81 us (2%)
    ppermute x8, starting transfers between devices, along(): return lax.ppermute(value, 'db', pairs)  13.7 us
    pallas_call x1, Pallas kernels, local(): pl.pallas_call(score_kernel, out_shape=[jax.ShapeDtypeStruct((rows, featu...  7.77 us
    pallas_call x4, Pallas kernels, sums(): pl.pallas_call(functools.partial(sums_kernel, len(blocks), part), out_sha...  7.49 us
    ppermute x5, waiting for transfers between devices, swap(): return lax.ppermute(value, 'db', [(i, i ^ 1) for i in range(owners)])  4.36 us
    ppermute x4, starting transfers between devices, cross(): return lax.ppermute(value, ('pb', 'db'), pairs)  4.33 us
    ppermute x8, waiting for transfers between devices, along(): return lax.ppermute(value, 'db', pairs)  3.57 us
    pallas_call x1, Pallas kernels, local(): pl.pallas_call(functools.partial(count_kernel, planes), out_shape=[jax.Sh...  3 us
    pallas_call x2, Pallas kernels, late(): pl.pallas_call(functools.partial(late_kernel, number), out_shape=jax.Shap...  1.65 us
  transfers between devices with their start and end apart: 17, of which 7 were waited for; matrix products, arithmetic and copies ran while one was open for 4% of the time, Pallas kernels for 22%

profile of v1, /device:TPU:0, one launch (start us, length us, event | category | flops | bytes accessed | tf_op | source)
XLA Modules:
  0.0 51.5 jit_solution(1323096560192138358)
XLA Ops:
  0.6 0.5 %collective-permute-start.1 = (bf16[256,768]{1,0:T(8,128)(2,1)}, bf16[256,768]{1,0:T(8,128)(2,1)S(1)}, u32[]{:S(2)}, u32[]{:S(2)}) collective-permute-start(bf16[256,768]{1,0:T(8,128)(2,1)} %database_ref.1), channel_id=1, source_target_pairs={{0,1},{1,0},{2,3},{3,2},{4,5},{5,4},{6,7},{7,6},{8,9},{9,8},{10,11... | collective-permute-start | bytes 1179656 | tf_op jit(solution)/shard_map/ppermute | solution.py:231
  1.1 0.9 %constant_dynamic-slice_fusion = bf16[64,768]{1,0:T(8,128)(2,1)S(1)} fusion(bf16[256,768]{1,0:T(8,128)(2,1)} %database_ref.1, s32[]{:T(128)S(6)} %select_n.27), kind=kLoop, calls=%fused_computation.6 | loop fusion | bytes 196612 | tf_op jit(solution)/shard_map/dynamic_slice | solution.py:240
  2.0 2.6 %collective-permute-start.2 = (bf16[64,768]{1,0:T(8,128)(2,1)S(1)}, bf16[64,768]{1,0:T(8,128)(2,1)S(1)}, u32[]{:S(2)}, u32[]{:S(2)}) collective-permute-start(bf16[64,768]{1,0:T(8,128)(2,1)S(1)} %constant_dynamic-slice_fusion), channel_id=1, source_target_pairs={{0,2},{1,3},{2,0},{3,1},{4,6},{5,7},{6,4},{7,5},{8,10},{9,11},{10,... | collective-permute-start | bytes 294920 | tf_op jit(solution)/shard_map/ppermute | solution.py:228
  4.6 2.6 %collective-permute-start.3 = (bf16[64,768]{1,0:T(8,128)(2,1)S(1)}, bf16[64,768]{1,0:T(8,128)(2,1)S(1)}, u32[]{:S(2)}, u32[]{:S(2)}) collective-permute-start(bf16[64,768]{1,0:T(8,128)(2,1)S(1)} %constant_dynamic-slice_fusion), channel_id=1, source_target_pairs={{0,4},{1,5},{2,6},{3,7},{4,0},{5,1},{6,2},{7,3},{8,12},{9,13},{10,... | collective-permute-start | bytes 294920 | tf_op jit(solution)/shard_map/ppermute | solution.py:228
  7.2 0.7 %fusion = s32[256,16]{0,1:T(8,128)S(1)} fusion(s32[256,16]{0,1:T(8,128)} %param.5, s32[256]{0:T(256)} %param.6), kind=kLoop, calls=%fused_computation.3 | loop fusion | flops 8192 | bytes 33792 | tf_op jit(solution)/shard_map/jit(_where)/select_n | solution.py:245
  8.0 0.1 copy.7
  8.1 0.1 reshape.11.own_ref
  8.3 1.2 %collective-permute-done.twin_ref = s32[32,128]{1,0:T(8,128)S(1)} collective-permute-done((s32[32,128]{1,0:T(8,128)S(1)}, s32[32,128]{1,0:T(8,128)S(1)}, u32[]{:S(2)}, u32[]{:S(2)}) %collective-permute-start) | collective-permute-done | bytes 16416 | tf_op jit(solution)/shard_map/ppermute | solution.py:231
  9.4 1.0 %copy-done = bf16[256,768]{1,0:T(8,128)(2,1)S(1)} copy-done((bf16[256,768]{1,0:T(8,128)(2,1)S(1)}, bf16[256,768]{1,0:T(8,128)(2,1)}, u32[]{:S(2)}) %copy-start) | copy-done | bytes 393240
  10.4 3.0 %counts.1 = (bf16[512,256]{1,0:T(8,128)(2,1)S(1)}, bf16[512,256]{1,0:T(8,128)(2,1)S(1)}, bf16[512,256]{1,0:T(8,128)(2,1)S(1)}, bf16[512,256]{1,0:T(8,128)(2,1)S(...) custom-call(s32[32,128]{1,0:T(8,128)S(1)} %collective-permute-done.twin_ref, ...), custom_call_target="tpu_custom_call" | custom-call | flops 67108864 | bytes 262144 | tf_op jit(solution)/shard_map/counts/pallas_call | solution.py:249
  13.4 2.4 %own_sums.1 = (f32[512,768]{1,0:T(8,128)S(1)}, bf16[2048,768]{1,0:T(8,128)(2,1)S(1)}) custom-call(bf16[256,768]{1,0:T(8,128)(2,1)S(1)} %collective-permute-done.1.twin_ref.dest_ref, bf16[256,768]{1,0:T(8,128)(2,1)S(1)} %get-tuple-element.19.own_ref.rest_0_.dest_ref, bf16[512,256]{1,0:T(8,128)(2,1)S(1)} %get-tuple-element.21.counts_ref, ...), custom_call_target="tpu_custom_call" | custom-call | flops 67108864 | bytes 262144 | tf_op jit(solution)/shard_map/own_sums/pallas_call | solution.py:284
  15.9 1.8 %collective-permute-start.7 = (bf16[96,768]{1,0:T(8,128)(2,1)S(1)}, bf16[96,768]{1,0:T(8,128)(2,1)S(1)}, u32[]{:S(2)}, u32[]{:S(2)}) collective-permute-start(bf16[96,768]{1,0:T(8,128)(2,1)S(1)} %get-tuple-element.25.rest_0_), channel_id=1, source_target_pairs={{0,8},{1,17},{2,10},{3,19},{4,12},{5,21},{6,14},{7,23},{8,0},{9,25... | collective-permute-start | bytes 442376 | tf_op jit(solution)/shard_map/ppermute | solution.py:238
  17.7 2.3 %collective-permute-start.10 = (bf16[128,768]{1,0:T(8,128)(2,1)S(1)}, bf16[128,768]{1,0:T(8,128)(2,1)S(1)}, u32[]{:S(2)}, u32[]{:S(2)}) collective-permute-start(bf16[128,768]{1,0:T(8,128)(2,1)S(1)} %get-tuple-element.30), channel_id=1, source_target_pairs={{0,4},{1,7},{2,6},{3,5},{4,0},{5,3},{6,2},{7,1},{8,12},{9,15},{10,... | collective-permute-start | bytes 589832 | tf_op jit(solution)/shard_map/ppermute | solution.py:228
  20.0 1.5 %collective-permute-start.8 = (bf16[96,768]{1,0:T(8,128)(2,1)S(1)}, bf16[96,768]{1,0:T(8,128)(2,1)S(1)}, u32[]{:S(2)}, u32[]{:S(2)}) collective-permute-start(bf16[96,768]{1,0:T(8,128)(2,1)S(1)} %get-tuple-element.25.rest_0_), channel_id=1, source_target_pairs={{0,16},{1,9},{2,18},{3,11},{4,20},{5,13},{6,22},{7,15},{8,24},{9,1... | collective-permute-start | bytes 442376 | tf_op jit(solution)/shard_map/ppermute | solution.py:238
  21.5 0.5 %collective-permute-start.5 = (bf16[96,768]{1,0:T(8,128)(2,1)S(1)}, bf16[96,768]{1,0:T(8,128)(2,1)S(1)}, u32[]{:S(2)}, u32[]{:S(2)}) collective-permute-start(bf16[96,768]{1,0:T(8,128)(2,1)S(1)} %get-tuple-element.23.rest_1_), channel_id=1, source_target_pairs={{0,8},{1,17},{2,10},{3,19},{4,12},{5,21},{6,14},{7,23},{8,0},{9,25... | collective-permute-start | bytes 442376 | tf_op jit(solution)/shard_map/ppermute | solution.py:238
  22.0 0.5 collective-permute-start.6
  22.6 1.9 %collective-permute-start.9 = (bf16[64,768]{1,0:T(8,128)(2,1)S(1)}, bf16[64,768]{1,0:T(8,128)(2,1)S(1)}, u32[]{:S(2)}, u32[]{:S(2)}) collective-permute-start(bf16[64,768]{1,0:T(8,128)(2,1)S(1)} %get-tuple-element.29), channel_id=1, source_target_pairs={{0,2},{1,3},{2,0},{3,1},{4,6},{5,7},{6,4},{7,5},{8,10},{9,11},{10,... | collective-permute-start | bytes 294920 | tf_op jit(solution)/shard_map/ppermute | solution.py:228
  24.5 2.8 %near_sums.1 = (f32[512,768]{1,0:T(8,128)S(1)}, bf16[2048,768]{1,0:T(8,128)(2,1)S(1)}) custom-call(bf16[256,768]{1,0:T(8,128)(2,1)S(1)} %collective-permute-done.1.twin_ref.dest_ref, bf16[256,768]{1,0:T(8,128)(2,1)S(1)} %get-tuple-element.19.own_ref.rest_0_.dest_ref, bf16[512,256]{1,0:T(8,128)(2,1)S(1)} %get-tuple-element.26.counts_ref, ...), custom_call_target="tpu_custom_call" | custom-call | flops 67108864 | bytes 262144 | tf_op jit(solution)/shard_map/near_sums/pallas_call | solution.py:284
  27.3 1.1 %first_sums.1.rest_2_ = f32[512,768]{1,0:T(8,128)S(1)} custom-call(bf16[256,768]{1,0:T(8,128)(2,1)S(1)} %collective-permute-done.1.twin_ref.dest_ref, bf16[256,768]{1,0:T(8,128)(2,1)S(1)} %get-tuple-element.19.own_ref.rest_0_.dest_ref, bf16[512,256]{1,0:T(8,128)(2,1)S(1)} %get-tuple-element.24.counts_ref, ...), custom_call_target="tpu_custom_call" | custom-call | flops 67108864 | bytes 262144 | tf_op jit(solution)/shard_map/first_sums/pallas_call | solution.py:284
  28.5 1.1 %second_sums.1.early_ref = f32[512,768]{1,0:T(8,128)S(1)} custom-call(bf16[256,768]{1,0:T(8,128)(2,1)S(1)} %collective-permute-done.1.twin_ref.dest_ref, bf16[256,768]{1,0:T(8,128)(2,1)S(1)} %get-tuple-element.19.own_ref.rest_0_.dest_ref, bf16[512,256]{1,0:T(8,128)(2,1)S(1)} %get-tuple-element.20.counts_ref, ...), custom_call_target="tpu_custom_call" | custom-call | flops 67108864 | bytes 262144 | tf_op jit(solution)/shard_map/second_sums/pallas_call | solution.py:284
  29.7 0.8 %late_sums.3.twin_a_ref = f32[256,768]{1,0:T(8,128)S(1)} custom-call(bf16[256,768]{1,0:T(8,128)(2,1)S(1)} %collective-permute-done.1.twin_ref.dest_ref, f32[512,768]{1,0:T(8,128)S(1)} %second_sums.1.early_ref, bf16[512,256]{1,0:T(8,128)(2,1)S(1)} %get-tuple-element.28.counts_ref, bf16[64,768]{1,0:T(8,128)(2,1)S(1)} %collective-permute-done.9.rest_0_, ...), custom_call_target="tpu_custom_call" | custom-call | tf_op jit(solution)/shard_map/late_sums/pallas_call | solution.py:314
  30.6 0.8 %late_sums.2.own_a_ref = f32[256,768]{1,0:T(8,128)S(1)} custom-call(bf16[256,768]{1,0:T(8,128)(2,1)S(1)} %get-tuple-element.19.own_ref.rest_0_.dest_ref, f32[512,768]{1,0:T(8,128)S(1)} %second_sums.1.early_ref, bf16[512,256]{1,0:T(8,128)(2,1)S(1)} %get-tuple-element.28.counts_ref, bf16[64,768]{1,0:T(8,128)(2,1)S(1)} %collective-permute-done.9.rest_0_, ...), custom_call_target="tpu_custom_call" | custom-call | tf_op jit(solution)/shard_map/late_sums/pallas_call | solution.py:314
  31.4 0.6 %collective-permute-start.12 = (f32[256,768]{1,0:T(8,128)S(1)}, f32[256,768]{1,0:T(8,128)S(1)}, u32[]{:S(2)}, u32[]{:S(2)}) collective-permute-start(f32[256,768]{1,0:T(8,128)S(1)} %late_sums.2.own_a_ref), channel_id=1, source_target_pairs={{0,1},{1,0},{2,3},{3,2},{4,5},{5,4},{6,7},{7,6},{8,9},{9,8},{10,11... | collective-permute-start | bytes 2359304 | tf_op jit(solution)/shard_map/ppermute | solution.py:231
  32.0 0.9 %collective-permute-done.11.own_b_ref = f32[256,768]{1,0:T(8,128)S(1)} collective-permute-done((f32[256,768]{1,0:T(8,128)S(1)}, f32[256,768]{1,0:T(8,128)S(1)}, u32[]{:S(2)}, u32[]{:S(2)}) %collective-permute-start.11) | collective-permute-done | bytes 786464 | tf_op jit(solution)/shard_map/ppermute | solution.py:231
  32.9 1.1 %collective-permute-done.12.twin_b_ref = f32[256,768]{1,0:T(8,128)S(1)} collective-permute-done((f32[256,768]{1,0:T(8,128)S(1)}, f32[256,768]{1,0:T(8,128)S(1)}, u32[]{:S(2)}, u32[]{:S(2)}) %collective-permute-start.12) | collective-permute-done | bytes 786464 | tf_op jit(solution)/shard_map/ppermute | solution.py:231
  34.0 7.8 %scores.1 = (bf16[256,768]{1,0:T(8,128)(2,1)}, f32[64,128]{1,0:T(8,128)S(1)}) custom-call(f32[256,768]{1,0:T(8,128)S(1)} %late_sums.2.own_a_ref, f32[256,768]{1,0:T(8,128)S(1)} %collective-permute-done.11.own_b_ref, f32[256,768]{1,0:T(8,128)S(1)} %late_sums.3.twin_a_ref, f32[256,768]{1,0:T(8,128)S(1)} %collective-permute-done.12.twin_b_ref, ...), custom_call_target="tpu_custom_call" | custom-call | flops 6442450944 | bytes 12582912 | tf_op jit(solution)/shard_map/scores/pallas_call | solution.py:329
  41.8 3.0 %collective-permute-start.13 = (f32[64,128]{1,0:T(8,128)S(1)}, f32[64,128]{1,0:T(8,128)S(1)}, u32[]{:S(2)}, u32[]{:S(2)}) collective-permute-start(f32[64,128]{1,0:T(8,128)S(1)} %get-tuple-element.35), channel_id=1, source_target_pairs={{0,6},{1,7},{2,4},{3,5},{4,2},{5,3},{6,0},{7,1},{8,14},{9,15},{10,... | collective-permute-start | bytes 98312 | tf_op jit(solution)/shard_map/ppermute | solution.py:228
  44.8 1.3 %collective-permute-start.15 = (f32[64,128]{1,0:T(8,128)S(1)}, f32[64,128]{1,0:T(8,128)S(1)}, u32[]{:S(2)}, u32[]{:S(2)}) collective-permute-start(f32[64,128]{1,0:T(8,128)S(1)} %get-tuple-element.35), channel_id=1, source_target_pairs={{0,2},{1,3},{2,0},{3,1},{4,6},{5,7},{6,4},{7,5},{8,10},{9,11},{10,... | collective-permute-start | bytes 98312 | tf_op jit(solution)/shard_map/ppermute | solution.py:228
  46.1 1.3 %collective-permute-done.13 = f32[64,128]{1,0:T(8,128)S(1)} collective-permute-done((f32[64,128]{1,0:T(8,128)S(1)}, f32[64,128]{1,0:T(8,128)S(1)}, u32[]{:S(2)}, u32[]{:S(2)}) %collective-permute-start.13) | collective-permute-done | bytes 32800 | tf_op jit(solution)/shard_map/ppermute | solution.py:228
  47.5 2.1 %collective-permute-done.14 = f32[64,128]{1,0:T(8,128)S(1)} collective-permute-done((f32[64,128]{1,0:T(8,128)S(1)}, f32[64,128]{1,0:T(8,128)S(1)}, u32[]{:S(2)}, u32[]{:S(2)}) %collective-permute-start.14) | collective-permute-done | bytes 32800 | tf_op jit(solution)/shard_map/ppermute | solution.py:228
  49.7 1.2 %collective-permute-done.16 = f32[64,128]{1,0:T(8,128)S(1)} collective-permute-done((f32[64,128]{1,0:T(8,128)S(1)}, f32[64,128]{1,0:T(8,128)S(1)}, u32[]{:S(2)}, u32[]{:S(2)}) %collective-permute-start.16) | collective-permute-done | bytes 32800 | tf_op jit(solution)/shard_map/ppermute | solution.py:231
  50.9 0.6 %maximum_bitcast_fusion = f32[16384]{0:T(1024)} fusion(f32[64,128]{1,0:T(8,128)S(1)} %get-tuple-element.37, f32[64,128]{1,0:T(8,128)S(1)} %get-tuple-element.36), kind=kLoop, calls=%fused_computation | loop fusion | flops 16384 | bytes 131072 | tf_op jit(solution)/shard_map/reshape | solution.py:351
  (20 shorter events, 0.4 us)
Async XLA Ops:
  0.6 12.8 %collective-permute-start.1 = (bf16[256,768]{1,0:T(8,128)(2,1)}, bf16[256,768]{1,0:T(8,128)(2,1)S(1)}, u32[]{:S(2)}, u32[]{:S(2)}) collective-permute-start(bf16[256,768]{1,0:T(8,128)(2,1)} %database_ref.1), channel_id=1, source_target_pairs={{0,1},{1,0},{2,3},{3,2},{4,5},{5,4},{6,7},{7,6},{8,9},{9,8},{10,11... | collective-permute-start | bytes 1179656 | tf_op jit(solution)/shard_map/ppermute | solution.py:231
  2.0 13.8 %collective-permute-start.2 = (bf16[64,768]{1,0:T(8,128)(2,1)S(1)}, bf16[64,768]{1,0:T(8,128)(2,1)S(1)}, u32[]{:S(2)}, u32[]{:S(2)}) collective-permute-start(bf16[64,768]{1,0:T(8,128)(2,1)S(1)} %constant_dynamic-slice_fusion), channel_id=1, source_target_pairs={{0,2},{1,3},{2,0},{3,1},{4,6},{5,7},{6,4},{7,5},{8,10},{9,11},{10,... | collective-permute-start | bytes 294920 | tf_op jit(solution)/shard_map/ppermute | solution.py:228
  4.6 11.2 %collective-permute-start.3 = (bf16[64,768]{1,0:T(8,128)(2,1)S(1)}, bf16[64,768]{1,0:T(8,128)(2,1)S(1)}, u32[]{:S(2)}, u32[]{:S(2)}) collective-permute-start(bf16[64,768]{1,0:T(8,128)(2,1)S(1)} %constant_dynamic-slice_fusion), channel_id=1, source_target_pairs={{0,4},{1,5},{2,6},{3,7},{4,0},{5,1},{6,2},{7,3},{8,12},{9,13},{10,... | collective-permute-start | bytes 294920 | tf_op jit(solution)/shard_map/ppermute | solution.py:228
  7.2 8.7 %collective-permute-start.4 = (bf16[64,768]{1,0:T(8,128)(2,1)S(1)}, bf16[64,768]{1,0:T(8,128)(2,1)S(1)}, u32[]{:S(2)}, u32[]{:S(2)}) collective-permute-start(bf16[64,768]{1,0:T(8,128)(2,1)S(1)} %constant_dynamic-slice_fusion), channel_id=1, source_target_pairs={{0,6},{1,7},{2,4},{3,5},{4,2},{5,3},{6,0},{7,1},{8,14},{9,15},{10,... | collective-permute-start | bytes 294920 | tf_op jit(solution)/shard_map/ppermute | solution.py:228
  8.2 1.2 %collective-permute-start = (s32[32,128]{1,0:T(8,128)S(1)}, s32[32,128]{1,0:T(8,128)S(1)}, u32[]{:S(2)}, u32[]{:S(2)}) collective-permute-start(s32[32,128]{1,0:T(8,128)S(1)} %reshape.11.own_ref), channel_id=1, source_target_pairs={{0,1},{1,0},{2,3},{3,2},{4,5},{5,4},{6,7},{7,6},{8,9},{9,8},{10,11... | collective-permute-start | bytes 49160 | tf_op jit(solution)/shard_map/ppermute | solution.py:231
  9.4 1.0 %copy-start = (bf16[256,768]{1,0:T(8,128)(2,1)S(1)}, bf16[256,768]{1,0:T(8,128)(2,1)}, u32[]{:S(2)}) copy-start(bf16[256,768]{1,0:T(8,128)(2,1)} %database_ref.1) | copy-start | bytes 1179652
  15.9 6.6 %collective-permute-start.7 = (bf16[96,768]{1,0:T(8,128)(2,1)S(1)}, bf16[96,768]{1,0:T(8,128)(2,1)S(1)}, u32[]{:S(2)}, u32[]{:S(2)}) collective-permute-start(bf16[96,768]{1,0:T(8,128)(2,1)S(1)} %get-tuple-element.25.rest_0_), channel_id=1, source_target_pairs={{0,8},{1,17},{2,10},{3,19},{4,12},{5,21},{6,14},{7,23},{8,0},{9,25... | collective-permute-start | bytes 442376 | tf_op jit(solution)/shard_map/ppermute | solution.py:238
  17.7 12.0 %collective-permute-start.10 = (bf16[128,768]{1,0:T(8,128)(2,1)S(1)}, bf16[128,768]{1,0:T(8,128)(2,1)S(1)}, u32[]{:S(2)}, u32[]{:S(2)}) collective-permute-start(bf16[128,768]{1,0:T(8,128)(2,1)S(1)} %get-tuple-element.30), channel_id=1, source_target_pairs={{0,4},{1,7},{2,6},{3,5},{4,0},{5,3},{6,2},{7,1},{8,12},{9,15},{10,... | collective-permute-start | bytes 589832 | tf_op jit(solution)/shard_map/ppermute | solution.py:228
  20.0 7.3 %collective-permute-start.8 = (bf16[96,768]{1,0:T(8,128)(2,1)S(1)}, bf16[96,768]{1,0:T(8,128)(2,1)S(1)}, u32[]{:S(2)}, u32[]{:S(2)}) collective-permute-start(bf16[96,768]{1,0:T(8,128)(2,1)S(1)} %get-tuple-element.25.rest_0_), channel_id=1, source_target_pairs={{0,16},{1,9},{2,18},{3,11},{4,20},{5,13},{6,22},{7,15},{8,24},{9,1... | collective-permute-start | bytes 442376 | tf_op jit(solution)/shard_map/ppermute | solution.py:238
  21.5 6.9 %collective-permute-start.5 = (bf16[96,768]{1,0:T(8,128)(2,1)S(1)}, bf16[96,768]{1,0:T(8,128)(2,1)S(1)}, u32[]{:S(2)}, u32[]{:S(2)}) collective-permute-start(bf16[96,768]{1,0:T(8,128)(2,1)S(1)} %get-tuple-element.23.rest_1_), channel_id=1, source_target_pairs={{0,8},{1,17},{2,10},{3,19},{4,12},{5,21},{6,14},{7,23},{8,0},{9,25... | collective-permute-start | bytes 442376 | tf_op jit(solution)/shard_map/ppermute | solution.py:238
  22.0 6.4 %collective-permute-start.6 = (bf16[96,768]{1,0:T(8,128)(2,1)S(1)}, bf16[96,768]{1,0:T(8,128)(2,1)S(1)}, u32[]{:S(2)}, u32[]{:S(2)}) collective-permute-start(bf16[96,768]{1,0:T(8,128)(2,1)S(1)} %get-tuple-element.23.rest_1_), channel_id=1, source_target_pairs={{0,16},{1,9},{2,18},{3,11},{4,20},{5,13},{6,22},{7,15},{8,24},{9,1... | collective-permute-start | bytes 442376 | tf_op jit(solution)/shard_map/ppermute | solution.py:238
  22.6 7.1 %collective-permute-start.9 = (bf16[64,768]{1,0:T(8,128)(2,1)S(1)}, bf16[64,768]{1,0:T(8,128)(2,1)S(1)}, u32[]{:S(2)}, u32[]{:S(2)}) collective-permute-start(bf16[64,768]{1,0:T(8,128)(2,1)S(1)} %get-tuple-element.29), channel_id=1, source_target_pairs={{0,2},{1,3},{2,0},{3,1},{4,6},{5,7},{6,4},{7,5},{8,10},{9,11},{10,... | collective-permute-start | bytes 294920 | tf_op jit(solution)/shard_map/ppermute | solution.py:228
  30.5 2.4 %collective-permute-start.11 = (f32[256,768]{1,0:T(8,128)S(1)}, f32[256,768]{1,0:T(8,128)S(1)}, u32[]{:S(2)}, u32[]{:S(2)}) collective-permute-start(f32[256,768]{1,0:T(8,128)S(1)} %late_sums.3.twin_a_ref), channel_id=1, source_target_pairs={{0,1},{1,0},{2,3},{3,2},{4,5},{5,4},{6,7},{7,6},{8,9},{9,8},{10,11... | collective-permute-start | bytes 2359304 | tf_op jit(solution)/shard_map/ppermute | solution.py:231
  31.4 2.6 %collective-permute-start.12 = (f32[256,768]{1,0:T(8,128)S(1)}, f32[256,768]{1,0:T(8,128)S(1)}, u32[]{:S(2)}, u32[]{:S(2)}) collective-permute-start(f32[256,768]{1,0:T(8,128)S(1)} %late_sums.2.own_a_ref), channel_id=1, source_target_pairs={{0,1},{1,0},{2,3},{3,2},{4,5},{5,4},{6,7},{7,6},{8,9},{9,8},{10,11... | collective-permute-start | bytes 2359304 | tf_op jit(solution)/shard_map/ppermute | solution.py:231
  41.8 5.7 %collective-permute-start.13 = (f32[64,128]{1,0:T(8,128)S(1)}, f32[64,128]{1,0:T(8,128)S(1)}, u32[]{:S(2)}, u32[]{:S(2)}) collective-permute-start(f32[64,128]{1,0:T(8,128)S(1)} %get-tuple-element.35), channel_id=1, source_target_pairs={{0,6},{1,7},{2,4},{3,5},{4,2},{5,3},{6,0},{7,1},{8,14},{9,15},{10,... | collective-permute-start | bytes 98312 | tf_op jit(solution)/shard_map/ppermute | solution.py:228
  44.8 4.8 %collective-permute-start.14 = (f32[64,128]{1,0:T(8,128)S(1)}, f32[64,128]{1,0:T(8,128)S(1)}, u32[]{:S(2)}, u32[]{:S(2)}) collective-permute-start(f32[64,128]{1,0:T(8,128)S(1)} %get-tuple-element.35), channel_id=1, source_target_pairs={{0,4},{1,5},{2,6},{3,7},{4,0},{5,1},{6,2},{7,3},{8,12},{9,13},{10,... | collective-permute-start | bytes 98312 | tf_op jit(solution)/shard_map/ppermute | solution.py:228
  44.8 4.8 %collective-permute-start.15 = (f32[64,128]{1,0:T(8,128)S(1)}, f32[64,128]{1,0:T(8,128)S(1)}, u32[]{:S(2)}, u32[]{:S(2)}) collective-permute-start(f32[64,128]{1,0:T(8,128)S(1)} %get-tuple-element.35), channel_id=1, source_target_pairs={{0,2},{1,3},{2,0},{3,1},{4,6},{5,7},{6,4},{7,5},{8,10},{9,11},{10,... | collective-permute-start | bytes 98312 | tf_op jit(solution)/shard_map/ppermute | solution.py:228
  49.6 1.3 %collective-permute-start.16 = (f32[64,128]{1,0:T(8,128)S(1)}, f32[64,128]{1,0:T(8,128)S(1)}, u32[]{:S(2)}, u32[]{:S(2)}) collective-permute-start(f32[64,128]{1,0:T(8,128)S(1)} %maximum_maximum_fusion), channel_id=1, source_target_pairs={{0,1},{1,0},{2,3},{3,2},{4,5},{5,4},{6,7},{7,6},{8,9},{9,8},{10,11... | collective-permute-start | bytes 98312 | tf_op jit(solution)/shard_map/ppermute | solution.py:231
